TPU v7x, 512 devices: a whole 4x8x8 slice. The times are simulated.
512 devices in a mesh: ctx: 256 (over z, y, x), uly: 2 (over core).
Axes of the slice: x: 4, y: 8, z: 8, core: 2. Of those that a mesh axis runs over, the one named last changes fastest.
Arguments:
- queries: bfloat16 [65536, 2048], P(('ctx', 'uly')), may hold values from -8 to 8
- keys: bfloat16 [65536, 512], P(('ctx', 'uly')), may hold values from -3 to 3
- values: bfloat16 [65536, 512], P(('ctx', 'uly')), may hold values from -6 to 6
- output_gradient: bfloat16 [65536, 2048], P(('ctx', 'uly')), may hold values from -6 to 6
- segment_ids: int32 [65536], replicated, may hold values from 0 to 255, never falling along the last dimension, each value on 1 to 513 neighbouring positions
Outputs:
- attn_out: bfloat16 [65536, 2048], P(('ctx', 'uly'))
- query_grad: bfloat16 [65536, 2048], P(('ctx', 'uly'))
- key_gradient: bfloat16 [65536, 512], P(('ctx', 'uly'))
- value_gradient: bfloat16 [65536, 512], P(('ctx', 'uly'))
Inputs may be any that keep to these rules, and one draw needn't show every extreme that they name: `segment_ids`: segment numbers never fall along the window; each document holds 1 to 513 consecutive tokens, and one holds exactly 513.
All inputs are finite; a program needn't handle non-finite values.
Results may differ from a plain program's by a relative error of at most 0.03.
Values may be sent and summed in bfloat16 or wider, within the bound.
A program may use at most 64 MiB of HBM per device.

v0:
```python
import jax
import jax.numpy as jnp
from jax import lax
from jax.sharding import PartitionSpec as P

QUERY_HEADS = 16
KEY_VALUE_HEADS = 4
HEAD_SIZE = 128
REACH = 2


def passed_along(value, axis, steps):
    count = lax.axis_size(axis)
    first, last = (max(0, -steps), min(count, count - steps))
    return lax.ppermute(value, axis, [(source, source + steps) for source in range(first, last)])


def for_sending(x):

    def short(part):
        return part.astype(jnp.bfloat16) if part.dtype == jnp.float32 else part

    return jax.tree.map(short, x)


def head_scores(query_group, key_rows, allowed):
    raw_scores = jnp.einsum(
        "qgd,kd->gqk", query_group, key_rows, preferred_element_type=jnp.float32
    ) * HEAD_SIZE ** (-0.5)
    return jnp.where(allowed, raw_scores, -1e30)


def per_device(queries, keys, values, output_gradient, segment_ids):
    query_heads, key_heads, value_heads, grad_heads = (
        lax.all_to_all(queries, "uly", split_axis=1, concat_axis=0, tiled=True),
        lax.all_to_all(keys, "uly", split_axis=1, concat_axis=0, tiled=True),
        lax.all_to_all(values, "uly", split_axis=1, concat_axis=0, tiled=True),
        lax.all_to_all(output_gradient, "uly", split_axis=1, concat_axis=0, tiled=True),
    )
    shard_len = query_heads.shape[0]
    local_groups = key_heads.shape[1] // HEAD_SIZE
    group_width = QUERY_HEADS // KEY_VALUE_HEADS
    shard_index = lax.axis_index("ctx")
    padded_ids = jnp.concatenate([jnp.full((REACH * shard_len,), -1, jnp.int32), segment_ids])
    query_ids = lax.dynamic_slice_in_dim(padded_ids, (shard_index + REACH) * shard_len, shard_len)
    stacked = jnp.stack([key_heads, value_heads])
    key_blocks = [stacked]
    received = stacked
    for distance in range(1, REACH + 1):
        received = passed_along(received, "ctx", 1)
        key_blocks.append(received)
    lower = jnp.arange(shard_len)[None, :] <= jnp.arange(shard_len)[:, None]
    masks = []
    for distance in range(REACH + 1):
        key_ids = lax.dynamic_slice_in_dim(
            padded_ids, (shard_index + REACH - distance) * shard_len, shard_len
        )
        allowed = query_ids[:, None] == key_ids[None, :]
        if distance == 0:
            allowed = allowed & lower
        masks.append(allowed[None])
    out_parts = []
    query_parts = []
    key_parts = [[] for distance in range(REACH + 1)]
    value_parts = [[] for distance in range(REACH + 1)]
    for group_index in range(local_groups):
        wide = slice(
            group_index * group_width * HEAD_SIZE, (group_index + 1) * group_width * HEAD_SIZE
        )
        narrow = slice(group_index * HEAD_SIZE, (group_index + 1) * HEAD_SIZE)
        query_group = query_heads[:, wide].reshape(shard_len, group_width, HEAD_SIZE)
        grad_group = grad_heads[:, wide].reshape(shard_len, group_width, HEAD_SIZE)
        scores = [
            head_scores(query_group, key_blocks[distance][0][:, narrow], masks[distance])
            for distance in range(REACH + 1)
        ]
        highest = jnp.max(scores[0], axis=-1)
        for distance in range(1, REACH + 1):
            highest = jnp.maximum(highest, jnp.max(scores[distance], axis=-1))
        total = jnp.zeros_like(highest)
        for distance in range(REACH + 1):
            total = total + jnp.sum(jnp.exp(scores[distance] - highest[..., None]), axis=-1)
        logsum = highest + jnp.log(total)
        probs = [jnp.exp(scores[distance] - logsum[..., None]) for distance in range(REACH + 1)]
        rounded = [weights.astype(jnp.bfloat16) for weights in probs]
        output = jnp.zeros((shard_len, group_width, HEAD_SIZE), jnp.float32)
        for distance in range(REACH + 1):
            output = output + jnp.einsum(
                "gqk,kd->qgd",
                rounded[distance],
                key_blocks[distance][1][:, narrow],
                preferred_element_type=jnp.float32,
            )
        output = output.astype(jnp.bfloat16)
        out_parts.append(output.reshape(shard_len, group_width * HEAD_SIZE))
        delta = jnp.transpose(
            jnp.sum(grad_group.astype(jnp.float32) * output.astype(jnp.float32), axis=-1)
        )
        query_total = jnp.zeros((shard_len, group_width, HEAD_SIZE), jnp.float32)
        for distance in range(REACH + 1):
            key_rows = key_blocks[distance][0][:, narrow]
            value_rows = key_blocks[distance][1][:, narrow]
            value_parts[distance].append(
                jnp.einsum(
                    "gqk,qgd->kd", rounded[distance], grad_group, preferred_element_type=jnp.float32
                )
            )
            dprob = jnp.einsum(
                "qgd,kd->gqk", grad_group, value_rows, preferred_element_type=jnp.float32
            )
            dscore = (probs[distance] * (dprob - delta[..., None])).astype(jnp.bfloat16)
            query_total = query_total + jnp.einsum(
                "gqk,kd->qgd", dscore, key_rows, preferred_element_type=jnp.float32
            ) * HEAD_SIZE ** (-0.5)
            key_parts[distance].append(
                jnp.einsum("gqk,qgd->kd", dscore, query_group, preferred_element_type=jnp.float32)
                * HEAD_SIZE ** (-0.5)
            )
        query_parts.append(
            query_total.astype(jnp.bfloat16).reshape(shard_len, group_width * HEAD_SIZE)
        )
    out_heads = jnp.concatenate(out_parts, axis=1)
    out_tokens = lax.all_to_all(out_heads, "uly", split_axis=0, concat_axis=1, tiled=True)
    partials = [
        jnp.stack(
            [
                jnp.concatenate(key_parts[distance], axis=1),
                jnp.concatenate(value_parts[distance], axis=1),
            ]
        )
        for distance in range(REACH + 1)
    ]
    summed = partials[0]
    running = jnp.zeros_like(summed)
    for distance in range(REACH, 0, -1):
        running = passed_along(for_sending(running + partials[distance]), "ctx", -1)
    summed = summed + running
    query_heads_grad = jnp.concatenate(query_parts, axis=1)
    key_heads_grad = summed[0].astype(jnp.bfloat16)
    value_heads_grad = summed[1].astype(jnp.bfloat16)
    query_grad, key_gradient, value_gradient = (
        lax.all_to_all(query_heads_grad, "uly", split_axis=0, concat_axis=1, tiled=True),
        lax.all_to_all(key_heads_grad, "uly", split_axis=0, concat_axis=1, tiled=True),
        lax.all_to_all(value_heads_grad, "uly", split_axis=0, concat_axis=1, tiled=True),
    )
    return (out_tokens, query_grad, key_gradient, value_gradient)


def solution(mesh):
    placed = (
        P(("ctx", "uly"), None),
        P(("ctx", "uly"), None),
        P(("ctx", "uly"), None),
        P(("ctx", "uly"), None),
        P(),
    )
    return jax.shard_map(
        per_device,
        mesh=mesh,
        in_specs=placed,
        out_specs=(
            P(("ctx", "uly"), None),
            P(("ctx", "uly"), None),
            P(("ctx", "uly"), None),
            P(("ctx", "uly"), None),
        ),
        check_vma=False,
    )
```

profile of v0, /device:TPU:255, one launch (start us, length us, event | category | flops | bytes accessed | tf_op | source)
XLA Modules:
  0.0 116.0 jit_solution(6960070708178465528)
XLA Ops:
  0.6 1.6 %copy.403 = bf16[16,2,8,256]{3,2,0,1:T(8,128)(2,1)} copy(bf16[16,2,8,256]{3,2,1,0:T(8,128)(2,1)} %bitcast.394) | data formatting | bytes 262144 | tf_op jit(solution)/shard_map/all_to_all | solution.py:36
  2.2 4.2 %all-to-all-start = ((bf16[128,2,256]{2,0,1:T(8,128)(2,1)}), bf16[128,2,256]{2,0,1:T(8,128)(2,1)S(1)}, u32[]{:S(2)}, u32[]{:S(2)}) async-start(bf16[128,2,256]{2,0,1:T(8,128)(2,1)} %bitcast.348), calls=%async_computation | async-start | bytes 262144 | tf_op jit(solution)/shard_map/all_to_all | solution.py:36
  6.4 1.1 all-to-all-done
  7.5 3.8 %all_to_all.140 = bf16[128,2,256]{2,0,1:T(8,128)(2,1)S(1)} all-to-all(bf16[128,2,256]{2,0,1:T(8,128)(2,1)S(1)} %bitcast.391), channel_id=1, replica_groups=mesh['ctx'=256,'uly'=2] {'uly'}, dimensions={1} | all-to-all | bytes 262144 | tf_op jit(solution)/shard_map/all_to_all | solution.py:37
  12.0 4.3 %collective-permute-start = (bf16[2,256,256]{2,1,0:T(8,128)(2,1)}, bf16[2,256,256]{2,1,0:T(8,128)(2,1)}, u32[]{:S(2)}, u32[]{:S(2)}) collective-permute-start(bf16[2,256,256]{2,1,0:T(8,128)(2,1)} %pad_maximum_fusion.2), channel_id=1, source_target_pairs={{0,2},{2,4},{4,6},{6,8},{8,10},{10,12},{12,14},{14,16},{16,18},{18... | collective-permute-start | bytes 786440 | tf_op jit(solution)/shard_map/ppermute | solution.py:15
  17.4 4.2 %all-to-all-start.1 = ((bf16[128,2,1024]{0,2,1:T(8,128)(2,1)}), bf16[128,2,1024]{0,2,1:T(8,128)(2,1)S(1)}, u32[]{:S(2)}, u32[]{:S(2)}) async-start(bf16[128,2,1024]{0,2,1:T(8,128)(2,1)} %bitcast.3), calls=%async_computation.1 | async-start | bytes 1048576 | tf_op jit(solution)/shard_map/all_to_all | solution.py:35
  23.0 3.9 %all-to-all-start.4 = ((bf16[128,2,1024]{2,0,1:T(8,128)(2,1)}), bf16[128,2,1024]{2,0,1:T(8,128)(2,1)S(1)}, u32[]{:S(2)}, u32[]{:S(2)}) async-start(bf16[128,2,1024]{2,0,1:T(8,128)(2,1)} %copy.288), calls=%async_computation.4 | async-start | bytes 1048576 | tf_op jit(solution)/shard_map/all_to_all | solution.py:38
  29.4 1.2 fusion.86
  31.6 3.3 %collective-permute-start.1 = (bf16[2,256,256]{2,1,0:T(8,128)(2,1)}, bf16[2,256,256]{2,1,0:T(8,128)(2,1)S(1)}, u32[]{:S(2)}, u32[]{:S(2)}) collective-permute-start(bf16[2,256,256]{2,1,0:T(8,128)(2,1)} %collective-permute-done), channel_id=1, source_target_pairs={{0,2},{2,4},{4,6},{6,8},{8,10},{10,12},{12,14},{14,16},{16,18},{18... | collective-permute-start | bytes 786440 | tf_op jit(solution)/shard_map/ppermute | solution.py:15
  35.5 6.1 %collective-permute-done.1 = bf16[2,256,256]{2,1,0:T(8,128)(2,1)S(1)} collective-permute-done((bf16[2,256,256]{2,1,0:T(8,128)(2,1)}, bf16[2,256,256]{2,1,0:T(8,128)(2,1)S(1)}, u32[]{:S(2)}, u32[]{:S(2)}) %collective-permute-start.1) | collective-permute-done | bytes 262176 | tf_op jit(solution)/shard_map/ppermute | solution.py:15
  46.3 1.0 multiply_reduce_fusion
  52.7 1.0 multiply_reduce_fusion.1
  54.1 1.1 fusion.27
  60.0 1.7 %copy.286 = bf16[2,128,512]{1,2,0:T(8,128)(2,1)} copy(bf16[2,128,512]{1,0,2:T(2,128)(2,1)} %concatenate.41) | data formatting | bytes 524288 | tf_op jit(solution)/shard_map/concatenate | solution.py:122
  67.8 4.4 %all-to-all-start.5 = ((bf16[2,128,1024]{2,1,0:T(8,128)(2,1)}), bf16[2,128,1024]{2,1,0:T(8,128)(2,1)S(1)}, u32[]{:S(2)}, u32[]{:S(2)}) async-start(bf16[2,128,1024]{2,1,0:T(8,128)(2,1)} %pad_maximum_fusion.1), calls=%async_computation.5 | async-start | bytes 1048576 | tf_op jit(solution)/shard_map/all_to_all | solution.py:142
  74.0 2.1 %collective-permute-start.2 = (bf16[2,256,256]{1,2,0:T(8,128)(2,1)}, bf16[2,256,256]{1,2,0:T(8,128)(2,1)}, u32[]{:S(2)}, u32[]{:S(2)}) collective-permute-start(bf16[2,256,256]{1,2,0:T(8,128)(2,1)} %pad_maximum_fusion.3), channel_id=1, source_target_pairs={{2,0},{4,2},{6,4},{8,6},{10,8},{12,10},{14,12},{16,14},{18,16},{20... | collective-permute-start | bytes 786440 | tf_op jit(solution)/shard_map/ppermute | solution.py:15
  77.9 2.0 %copy.331 = bf16[128,2048]{1,0:T(8,128)(2,1)} copy(bf16[128,2048]{0,1:T(8,128)(2,1)} %bitcast.383) | data formatting | bytes 1048576
  79.9 3.8 %all_to_all.141 = bf16[2,128,1024]{1,2,0:T(8,128)(2,1)S(1)} all-to-all(bf16[2,128,1024]{1,2,0:T(8,128)(2,1)S(1)} %pad_maximum_fusion), channel_id=1, replica_groups=mesh['ctx'=256,'uly'=2] {'uly'}, dimensions={0} | all-to-all | bytes 1048576 | tf_op jit(solution)/shard_map/all_to_all | solution.py:123
  85.0 4.6 %collective-permute-done.2 = bf16[2,256,256]{1,2,0:T(8,128)(2,1)} collective-permute-done((bf16[2,256,256]{1,2,0:T(8,128)(2,1)}, bf16[2,256,256]{1,2,0:T(8,128)(2,1)}, u32[]{:S(2)}, u32[]{:S(2)}) %collective-permute-start.2) | collective-permute-done | bytes 262176 | tf_op jit(solution)/shard_map/ppermute | solution.py:15
  89.7 1.0 fusion.65
  90.7 2.1 %collective-permute-start.3 = (bf16[2,256,256]{1,2,0:T(8,128)(2,1)S(1)}, bf16[2,256,256]{1,2,0:T(8,128)(2,1)S(1)}, u32[]{:S(2)}, u32[]{:S(2)}) collective-permute-start(bf16[2,256,256]{1,2,0:T(8,128)(2,1)S(1)} %fusion.65), channel_id=1, source_target_pairs={{2,0},{4,2},{6,4},{8,6},{10,8},{12,10},{14,12},{16,14},{18,16},{20... | collective-permute-start | bytes 786440 | tf_op jit(solution)/shard_map/ppermute | solution.py:15
  93.2 12.0 %collective-permute-done.3 = bf16[2,256,256]{1,2,0:T(8,128)(2,1)S(1)} collective-permute-done((bf16[2,256,256]{1,2,0:T(8,128)(2,1)S(1)}, bf16[2,256,256]{1,2,0:T(8,128)(2,1)S(1)}, u32[]{:S(2)}, u32[]{:S(2)}) %collective-permute-start.3) | collective-permute-done | bytes 262176 | tf_op jit(solution)/shard_map/ppermute | solution.py:15
  105.3 5.2 %all_to_all.142 = bf16[2,128,256]{1,2,0:T(8,128)(2,1)S(1)} all-to-all(bf16[2,128,256]{1,2,0:T(8,128)(2,1)S(1)} %copy.329), channel_id=1, replica_groups=mesh['ctx'=256,'uly'=2] {'uly'}, dimensions={0} | all-to-all | bytes 262144 | tf_op jit(solution)/shard_map/all_to_all | solution.py:144
  111.4 3.8 %all_to_all.143 = bf16[2,128,256]{1,2,0:T(8,128)(2,1)S(1)} all-to-all(bf16[2,128,256]{1,2,0:T(8,128)(2,1)S(1)} %copy.328), channel_id=1, replica_groups=mesh['ctx'=256,'uly'=2] {'uly'}, dimensions={0} | all-to-all | bytes 262144 | tf_op jit(solution)/shard_map/all_to_all | solution.py:143
  (131 shorter events, 35.2 us)
Async XLA Ops:
  2.2 4.2 %copy-start.24 = (bf16[128,512]{1,0:T(8,128)(2,1)S(1)}, bf16[128,512]{1,0:T(8,128)(2,1)}, u32[]{:S(2)}) copy-start(bf16[128,512]{1,0:T(8,128)(2,1)} %param.7) | copy-start | bytes 393220
  2.2 5.3 %all-to-all-start = ((bf16[128,2,256]{2,0,1:T(8,128)(2,1)}), bf16[128,2,256]{2,0,1:T(8,128)(2,1)S(1)}, u32[]{:S(2)}, u32[]{:S(2)}) async-start(bf16[128,2,256]{2,0,1:T(8,128)(2,1)} %bitcast.348), calls=%async_computation | async-start | bytes 262144 | tf_op jit(solution)/shard_map/all_to_all | solution.py:36
  6.4 10.0 %copy-start.11 = (bf16[128,2048]{1,0:T(8,128)(2,1)S(1)}, bf16[128,2048]{1,0:T(8,128)(2,1)}, u32[]{:S(2)}) copy-start(bf16[128,2048]{1,0:T(8,128)(2,1)} %param.5) | copy-start | bytes 1572868
  12.0 18.5 %collective-permute-start = (bf16[2,256,256]{2,1,0:T(8,128)(2,1)}, bf16[2,256,256]{2,1,0:T(8,128)(2,1)}, u32[]{:S(2)}, u32[]{:S(2)}) collective-permute-start(bf16[2,256,256]{2,1,0:T(8,128)(2,1)} %pad_maximum_fusion.2), channel_id=1, source_target_pairs={{0,2},{2,4},{4,6},{6,8},{8,10},{10,12},{12,14},{14,16},{16,18},{18... | collective-permute-start | bytes 786440 | tf_op jit(solution)/shard_map/ppermute | solution.py:15
  17.4 4.2 %copy-start.12 = (bf16[128,2048]{1,0:T(8,128)(2,1)S(1)}, bf16[128,2048]{1,0:T(8,128)(2,1)}, u32[]{:S(2)}) copy-start(bf16[128,2048]{1,0:T(8,128)(2,1)} %param.8) | copy-start | bytes 1572868
  17.4 5.6 %all-to-all-start.1 = ((bf16[128,2,1024]{0,2,1:T(8,128)(2,1)}), bf16[128,2,1024]{0,2,1:T(8,128)(2,1)S(1)}, u32[]{:S(2)}, u32[]{:S(2)}) async-start(bf16[128,2,1024]{0,2,1:T(8,128)(2,1)} %bitcast.3), calls=%async_computation.1 | async-start | bytes 1048576 | tf_op jit(solution)/shard_map/all_to_all | solution.py:35
  23.0 6.0 %all-to-all-start.4 = ((bf16[128,2,1024]{2,0,1:T(8,128)(2,1)}), bf16[128,2,1024]{2,0,1:T(8,128)(2,1)S(1)}, u32[]{:S(2)}, u32[]{:S(2)}) async-start(bf16[128,2,1024]{2,0,1:T(8,128)(2,1)} %copy.288), calls=%async_computation.4 | async-start | bytes 1048576 | tf_op jit(solution)/shard_map/all_to_all | solution.py:38
  27.1 1.0 copy-start.19
  31.6 25.8 %copy-start.1 = (bf16[256,256]{1,0:T(8,128)(2,1)}, bf16[256,256]{1,0:T(8,128)(2,1)S(1)}, u32[]{:S(2)}) copy-start(bf16[256,256]{1,0:T(8,128)(2,1)S(1)} %get-tuple-element.31) | copy-start | bytes 393220
  31.6 10.0 %collective-permute-start.1 = (bf16[2,256,256]{2,1,0:T(8,128)(2,1)}, bf16[2,256,256]{2,1,0:T(8,128)(2,1)S(1)}, u32[]{:S(2)}, u32[]{:S(2)}) collective-permute-start(bf16[2,256,256]{2,1,0:T(8,128)(2,1)} %collective-permute-done), channel_id=1, source_target_pairs={{0,2},{2,4},{4,6},{6,8},{8,10},{10,12},{12,14},{14,16},{16,18},{18... | collective-permute-start | bytes 786440 | tf_op jit(solution)/shard_map/ppermute | solution.py:15
  41.6 16.1 %copy-start.3 = (bf16[256,256]{1,0:T(8,128)(2,1)}, bf16[256,256]{1,0:T(8,128)(2,1)S(1)}, u32[]{:S(2)}) copy-start(bf16[256,256]{1,0:T(8,128)(2,1)S(1)} %get-tuple-element.29) | copy-start | bytes 393220
  59.2 2.5 %copy-start = (bf16[4,256,256]{1,2,0:T(8,128)(2,1)S(1)}, bf16[4,256,256]{1,2,0:T(8,128)(2,1)}, u32[]{:S(2)}) copy-start(bf16[4,256,256]{1,2,0:T(8,128)(2,1)} %fusion.27) | copy-start | bytes 1572868
  67.8 4.4 %copy-start.6 = (bf16[256,4,128]{0,2,1:T(8,128)(2,1)S(1)}, bf16[256,4,128]{0,2,1:T(8,128)(2,1)}, u32[]{:S(2)}) copy-start(bf16[256,4,128]{0,2,1:T(8,128)(2,1)} %get-tuple-element.53) | copy-start | bytes 786436
  67.8 9.1 %all-to-all-start.5 = ((bf16[2,128,1024]{2,1,0:T(8,128)(2,1)}), bf16[2,128,1024]{2,1,0:T(8,128)(2,1)S(1)}, u32[]{:S(2)}, u32[]{:S(2)}) async-start(bf16[2,128,1024]{2,1,0:T(8,128)(2,1)} %pad_maximum_fusion.1), calls=%async_computation.5 | async-start | bytes 1048576 | tf_op jit(solution)/shard_map/all_to_all | solution.py:142
  73.2 2.8 %copy-start.7 = (bf16[2,128,512]{1,2,0:T(8,128)(2,1)S(1)}, bf16[2,128,512]{1,2,0:T(8,128)(2,1)}, u32[]{:S(2)}) copy-start(bf16[2,128,512]{1,2,0:T(8,128)(2,1)} %copy.286) | copy-start | bytes 786436
  74.0 2.1 %copy-start.14 = (f32[256,128]{0,1:T(8,128)S(1)}, f32[256,128]{0,1:T(8,128)}, u32[]{:S(2)}) copy-start(f32[256,128]{0,1:T(8,128)} %fusion.53) | copy-start | bytes 393220
  74.0 2.1 %copy-start.15 = (f32[256,128]{0,1:T(8,128)S(1)}, f32[256,128]{0,1:T(8,128)}, u32[]{:S(2)}) copy-start(f32[256,128]{0,1:T(8,128)} %fusion.52) | copy-start | bytes 393220
  74.0 2.1 %copy-start.17 = (f32[256,128]{0,1:T(8,128)S(1)}, f32[256,128]{0,1:T(8,128)}, u32[]{:S(2)}) copy-start(f32[256,128]{0,1:T(8,128)} %convolution_bitcast_fusion.12) | copy-start | bytes 393220
  74.0 2.2 %copy-start.18 = (f32[256,128]{0,1:T(8,128)S(1)}, f32[256,128]{0,1:T(8,128)}, u32[]{:S(2)}) copy-start(f32[256,128]{0,1:T(8,128)} %convolution_bitcast_fusion.13) | copy-start | bytes 393220
  74.0 15.7 %collective-permute-start.2 = (bf16[2,256,256]{1,2,0:T(8,128)(2,1)}, bf16[2,256,256]{1,2,0:T(8,128)(2,1)}, u32[]{:S(2)}, u32[]{:S(2)}) collective-permute-start(bf16[2,256,256]{1,2,0:T(8,128)(2,1)} %pad_maximum_fusion.3), channel_id=1, source_target_pairs={{2,0},{4,2},{6,4},{8,6},{10,8},{12,10},{14,12},{16,14},{18,16},{20... | collective-permute-start | bytes 786440 | tf_op jit(solution)/shard_map/ppermute | solution.py:15
  84.7 4.9 %copy-start.9 = (f32[1,256,256]{1,2,0:T(8,128)S(1)}, f32[1,256,256]{1,2,0:T(8,128)}, u32[]{:S(2)}) copy-start(f32[1,256,256]{1,2,0:T(8,128)} %get-tuple-element.57) | copy-start | bytes 786436
  90.7 2.4 %copy-start.13 = (f32[256,128]{0,1:T(8,128)S(1)}, f32[256,128]{0,1:T(8,128)}, u32[]{:S(2)}) copy-start(f32[256,128]{0,1:T(8,128)} %fusion.49) | copy-start | bytes 393220
  90.7 2.4 %copy-start.16 = (f32[256,128]{0,1:T(8,128)S(1)}, f32[256,128]{0,1:T(8,128)}, u32[]{:S(2)}) copy-start(f32[256,128]{0,1:T(8,128)} %convolution_bitcast_fusion.20) | copy-start | bytes 393220
  90.7 14.5 %collective-permute-start.3 = (bf16[2,256,256]{1,2,0:T(8,128)(2,1)S(1)}, bf16[2,256,256]{1,2,0:T(8,128)(2,1)S(1)}, u32[]{:S(2)}, u32[]{:S(2)}) collective-permute-start(bf16[2,256,256]{1,2,0:T(8,128)(2,1)S(1)} %fusion.65), channel_id=1, source_target_pairs={{2,0},{4,2},{6,4},{8,6},{10,8},{12,10},{14,12},{16,14},{18,16},{20... | collective-permute-start | bytes 786440 | tf_op jit(solution)/shard_map/ppermute | solution.py:15
  (9 other events, 7.8 us)
where the time goes:
time: 117 us; the launch traced here: 116 us
  starting transfers between devices  28.4 us (24%)
  waiting for transfers between devices  23.9 us (20%)
  matrix products  21 us (18%)
  local copies, waits for them, and re-layouts  19.5 us (17%)
  blocking collectives  16.6 us (14%)
  other arithmetic  5.33 us (5%)
  between operations  1.21 us (1%)
    ppermute x4, waiting for transfers between devices, passed_along(): lax.ppermute(value, axis, [(source, source + steps) for source in range(f...  22.7 us
    ppermute x4, starting transfers between devices, passed_along(): lax.ppermute(value, axis, [(source, source + steps) for source in range(f...  11.7 us
    unnamed x58, local copies, waits for them, and re-layouts  10.2 us
    all_to_all x1, blocking collectives, per_device(): lax.all_to_all(value_heads_grad, 'uly', split_axis=0, concat_axis=1, tile...  5.18 us
    dot_general x6, matrix products, per_device(): jnp.einsum('gqk,qgd->kd', rounded[distance], grad_group, preferred_elemen...  5.15 us
    dot_general x6, matrix products, per_device(): jnp.einsum('gqk,qgd->kd', dscore, query_group, preferred_element_type=jnp...  5.05 us
    all_to_all x1, starting transfers between devices, per_device(): lax.all_to_all(query_heads_grad, 'uly', split_axis=0, concat_axis=1, tile...  4.4 us
    all_to_all x1, starting transfers between devices, per_device(): lax.all_to_all(queries, 'uly', split_axis=1, concat_axis=0, tiled=True)  4.24 us
  transfers between devices with their start and end apart: 8, of which 5 were waited for; matrix products, arithmetic and copies ran while one was open for 10% of the time, Pallas kernels for 0%

commit v1 on v0

v1 whole, which is shorter than its diff:
```python
import functools
import math

import jax
import jax.numpy as jnp
from jax import lax
from jax.experimental import pallas as pl
from jax.experimental.pallas import tpu as pltpu
from jax.sharding import PartitionSpec as P

MESH = pl.DeviceIdType.MESH
HEAD = 128
BLOCK = 128
GROUP = 4
GROUP_WIDTH = GROUP * HEAD
LOCAL = 2
HALF = LOCAL * GROUP_WIDTH
REACH = 2
SPAN = 5
ROWS = SPAN * BLOCK
SCALE = HEAD ** -0.5
TO_EXP2 = SCALE * math.log2(math.e)
NONE = -1e30

f32 = jnp.float32
bf16 = jnp.bfloat16


def dot(a, b, ca, cb):
    return lax.dot_general(a, b, (((ca,), (cb,)), ((), ())), preferred_element_type=f32)


def kernel(chips, q_hbm, k_hbm, v_hbm, g_hbm, ids_hbm, o_hbm, dq_hbm, dk_ref, dv_ref,
           q_buf, g_buf, kv_buf, ids_buf, bias, acc, out_buf, part, got, grad_buf,
           own_sem, ids_sem, qs_send, qs_recv, kv_send, kv_recv, out_sem, out_recv, part_send, part_recv):
    c, u = lax.axis_index("ctx"), lax.axis_index("uly")
    other = 1 - u
    kv_hbm = (k_hbm, v_hbm)

    barrier = pltpu.get_barrier_semaphore()
    pl.semaphore_signal(barrier, inc=1, device_id=(c, other), device_id_type=MESH)
    for step in (1, 2):
        for t in (0, 1):
            @pl.when(c >= step)
            def _():
                pl.semaphore_signal(barrier, inc=1, device_id=(c - step, t), device_id_type=MESH)

            @pl.when(c + step < chips)
            def _():
                pl.semaphore_signal(barrier, inc=1, device_id=(c + step, t), device_id_type=MESH)

    def own_of(g):
        columns = pl.ds(pl.multiple_of(u * HALF + g * GROUP_WIDTH, GROUP_WIDTH), GROUP_WIDTH)
        narrow = pl.ds(pl.multiple_of((u * LOCAL + g) * HEAD, HEAD), HEAD)
        wide = [pltpu.make_async_copy(a.at[:, columns], b.at[u, g], own_sem.at[g, i])
                for i, (a, b) in enumerate(((q_hbm, q_buf), (g_hbm, g_buf)))]
        return wide + [pltpu.make_async_copy(kv_hbm[i].at[:, narrow], kv_buf.at[i, g, 4 + u], own_sem.at[g, 2 + i])
                       for i in range(2)]

    ids_copies = []
    for b in range(6):
        row = jnp.maximum(2 * c - 4 + b, 0)
        ids_copies.append(pltpu.make_async_copy(ids_hbm.at[pl.ds(row, 1)], ids_buf.at[b, pl.ds(0, 1)], ids_sem.at[b]))
    for copy in own_of(0) + ids_copies + own_of(1):
        copy.start()

    for step in (1, 2):
        for i in range(2):
            @pl.when(c < step)
            def _():
                for g in range(LOCAL):
                    for t in (0, 1):
                        kv_buf[i, g, 2 * (REACH - step) + t] = jnp.zeros((BLOCK, HEAD), bf16)

    heard = 1
    for step in (1, 2):
        heard = heard + 2 * jnp.where(c >= step, 1, 0) + 2 * jnp.where(c + step < chips, 1, 0)
    pl.semaphore_wait(barrier, heard)

    def halo(i, g, step, t):
        columns = pl.ds((t * LOCAL + g) * HEAD, HEAD)
        return pltpu.make_async_remote_copy(
            kv_hbm[i].at[:, columns], kv_buf.at[i, g, 2 * (REACH - step) + u],
            kv_send.at[i, g, step, t], kv_recv.at[i, g, step, u], device_id=(c + step, t), device_id_type=MESH)

    def swap_kv(i, g):
        columns = pl.ds(pl.multiple_of((other * LOCAL + g) * HEAD, HEAD), HEAD)
        return pltpu.make_async_remote_copy(
            kv_hbm[i].at[:, columns], kv_buf.at[i, g, 4 + u],
            kv_send.at[i, g, 0, 0], kv_recv.at[i, g, 0, 0], device_id=(c, other), device_id_type=MESH)

    def swap_q(i, g):
        columns = pl.ds(pl.multiple_of(other * HALF + g * GROUP_WIDTH, GROUP_WIDTH), GROUP_WIDTH)
        return pltpu.make_async_remote_copy(
            (q_hbm, g_hbm)[i].at[:, columns], (q_buf, g_buf)[i].at[u, g],
            qs_send.at[i, g], qs_recv.at[i, g], device_id=(c, other), device_id_type=MESH)

    for g in range(LOCAL):
        for step in (2, 1):
            @pl.when(c + step < chips)
            def _():
                for i in range(2):
                    for t in (0, 1):
                        halo(i, g, step, t).start()
        for i in range(2):
            swap_kv(i, g).start()
            swap_q(i, g).start()

    for copy in ids_copies:
        copy.wait()
    below = lax.broadcasted_iota(jnp.int32, (BLOCK, BLOCK), 0) <= lax.broadcasted_iota(jnp.int32, (BLOCK, BLOCK), 1)
    for b in range(6):
        key_ids = jnp.transpose(jnp.broadcast_to(ids_buf[b, 0:1, :], (BLOCK, BLOCK)))
        if b < 4:
            key_ids = jnp.where(c >= REACH - b // 2, key_ids, -1)
        for s in (0, 1):
            if not s <= b < s + SPAN:
                continue
            allowed = key_ids == jnp.broadcast_to(ids_buf[4 + s, 0:1, :], (BLOCK, BLOCK))
            if b == 4 + s:
                allowed = allowed & below
            bias[s, b - s] = jnp.where(allowed, 0.0, NONE)

    def out_local(i, s, g):
        columns = pl.ds(pl.multiple_of(u * HALF + g * GROUP_WIDTH, GROUP_WIDTH), GROUP_WIDTH)
        return pltpu.make_async_copy(out_buf.at[i, s, g], (o_hbm, dq_hbm)[i].at[:, columns], out_sem.at[i, 0, g])

    def out_remote(i, s, g):
        columns = pl.ds(pl.multiple_of(u * HALF + g * GROUP_WIDTH, GROUP_WIDTH), GROUP_WIDTH)
        return pltpu.make_async_remote_copy(
            out_buf.at[i, s, g], (o_hbm, dq_hbm)[i].at[:, columns],
            out_sem.at[i, 1, g], out_recv.at[i, g], device_id=(c, other), device_id_type=MESH)

    def partial(i, g, step, t):
        return pltpu.make_async_remote_copy(
            part.at[i, g, 2 * (REACH - step) + t], got.at[i, g, step, u],
            part_send.at[i, g, step, t], part_recv.at[i, g, step, u], device_id=(c - step, t), device_id_type=MESH)

    def partial_chip(i, g):
        return pltpu.make_async_remote_copy(
            part.at[i, g, 4 + other], got.at[i, g, 0, u],
            part_send.at[i, g, 0, 0], part_recv.at[i, g, 0, 0], device_id=(c, other), device_id_type=MESH)

    def tile(g, s):
        keys = kv_buf[0, g, pl.ds(s, SPAN)].reshape(ROWS, HEAD)
        vals = kv_buf[1, g, pl.ds(s, SPAN)].reshape(ROWS, HEAD)
        keys_t, vals_t = jnp.transpose(keys), jnp.transpose(vals)
        add = bias[s].reshape(ROWS, BLOCK)
        add = jnp.concatenate([add, add], axis=1)
        dk = jnp.zeros((ROWS, HEAD), f32)
        dv = jnp.zeros((ROWS, HEAD), f32)
        for pair in range(GROUP // 2):
            heads = [slice((2 * pair + h) * HEAD, (2 * pair + h + 1) * HEAD) for h in (0, 1)]
            qs = jnp.concatenate([q_buf[s, g, :, h] for h in heads], axis=0)
            gs = jnp.concatenate([g_buf[s, g, :, h] for h in heads], axis=0)
            scores = dot(keys, qs, 1, 1) * TO_EXP2 + add
            highest = jnp.max(scores, axis=0, keepdims=True)
            probs = jnp.exp2(scores - highest)
            probs = probs * (1.0 / jnp.sum(probs, axis=0, keepdims=True))
            rounded = probs.astype(bf16)
            dprobs = dot(vals, gs, 1, 1)
            delta = jnp.sum(probs * dprobs, axis=0, keepdims=True)
            dscores = (probs * (dprobs - delta)).astype(bf16)
            dv = dv + dot(rounded, gs, 1, 0)
            dk = dk + dot(dscores, qs, 1, 0)
            out_t = dot(vals_t, rounded, 1, 0)
            dq_t = dot(keys_t, dscores, 1, 0) * SCALE
            for h in (0, 1):
                out_buf[0, s, g, :, heads[h]] = jnp.transpose(out_t[:, h * BLOCK:(h + 1) * BLOCK]).astype(bf16)
                out_buf[1, s, g, :, heads[h]] = jnp.transpose(dq_t[:, h * BLOCK:(h + 1) * BLOCK]).astype(bf16)
        acc[0, pl.ds(s, SPAN)] += dk.reshape(SPAN, BLOCK, HEAD) * SCALE
        acc[1, pl.ds(s, SPAN)] += dv.reshape(SPAN, BLOCK, HEAD)

    def head(g, carry):
        for copy in own_of(g):
            copy.wait()
        for i in range(2):
            swap_kv(i, g).wait_recv()
            swap_q(i, g).wait_recv()
        for step in (1, 2):
            @pl.when(c >= step)
            def _():
                for i in range(2):
                    for t in (0, 1):
                        arrived(i, g, step, t).wait_recv()
        acc[...] = jnp.zeros(acc.shape, f32)
        tile(g, other)
        for i in range(2):
            out_remote(i, other, g).start()
        tile(g, u)
        for i in range(2):
            part[i, g] = acc[i].astype(bf16)
        for step in (2, 1):
            @pl.when(c >= step)
            def _():
                for i in range(2):
                    for t in (0, 1):
                        partial(i, g, step, t).start()
        for i in range(2):
            partial_chip(i, g).start()
            grad_buf[i, g, u] = acc[i, 4 + u]
            out_local(i, u, g).start()
        return carry

    def arrived(i, g, step, t):
        return pltpu.make_async_remote_copy(
            kv_hbm[i].at[:, pl.ds(0, HEAD)], kv_buf.at[i, g, 2 * (REACH - step) + t],
            kv_send.at[i, g, step, t], kv_recv.at[i, g, step, t], device_id=(c, other), device_id_type=MESH)

    def later(i, g, step, t):
        return pltpu.make_async_remote_copy(
            part.at[i, g, 0], got.at[i, g, step, t], part_send.at[i, g, step, t],
            part_recv.at[i, g, step, t], device_id=(c, other), device_id_type=MESH)

    lax.fori_loop(0, LOCAL, head, 0)

    for g in range(LOCAL):
        for i in range(2):
            partial_chip(i, g).wait_recv()
            grad_buf[i, g, other] = got[i, g, 0, other].astype(f32)
        for step in (1, 2):
            @pl.when(c + step < chips)
            def _():
                for i in range(2):
                    for t in (0, 1):
                        later(i, g, step, t).wait_recv()
                        grad_buf[i, g, t] += got[i, g, step, t].astype(f32)
        for i in range(2):
            for t in (0, 1):
                (dk_ref, dv_ref)[i][:, (t * LOCAL + g) * HEAD:(t * LOCAL + g + 1) * HEAD] = grad_buf[i, g, t].astype(bf16)

    for g in range(LOCAL):
        for i in range(2):
            out_remote(i, other, g).wait()
            out_local(i, u, g).wait()
            swap_kv(i, g).wait_send()
            swap_q(i, g).wait_send()
            partial_chip(i, g).wait_send()
        for step in (1, 2):
            @pl.when(c + step < chips)
            def _():
                for i in range(2):
                    for t in (0, 1):
                        halo(i, g, step, t).wait_send()

            @pl.when(c >= step)
            def _():
                for i in range(2):
                    for t in (0, 1):
                        partial(i, g, step, t).wait_send()


def deliver(a0, a1, a2, a3, b0, b1, b2, b3, sem):
    copies = [pltpu.make_async_copy(a, b, sem.at[i]) for i, (a, b) in enumerate(zip((a0, a1, a2, a3), (b0, b1, b2, b3)))]
    for copy in copies:
        copy.start()
    for copy in copies:
        copy.wait()


def solution(mesh):
    chips = mesh.shape["ctx"]
    tokens = P(("ctx", "uly"), None)

    def per_device(queries, keys, values, output_gradient, segment_ids):
        rows = queries.shape[0]
        wide = jax.ShapeDtypeStruct((rows, 2 * HALF), bf16)
        narrow = jax.ShapeDtypeStruct((rows, 2 * LOCAL * HEAD), bf16)
        anywhere = pl.BlockSpec(memory_space=pltpu.HBM)
        vmem = pl.BlockSpec(memory_space=pltpu.VMEM)
        dma = pltpu.SemaphoreType.DMA
        held = pl.pallas_call(
            functools.partial(kernel, chips),
            out_shape=(wide, wide, narrow, narrow),
            in_specs=[anywhere] * 5,
            out_specs=(anywhere, anywhere, vmem, vmem),
            scratch_shapes=[
                pltpu.VMEM((2, LOCAL, BLOCK, GROUP_WIDTH), bf16),
                pltpu.VMEM((2, LOCAL, BLOCK, GROUP_WIDTH), bf16),
                pltpu.VMEM((2, LOCAL, 6, BLOCK, HEAD), bf16),
                pltpu.VMEM((6, 8, BLOCK), jnp.int32),
                pltpu.VMEM((2, SPAN, BLOCK, BLOCK), f32),
                pltpu.VMEM((2, 6, BLOCK, HEAD), f32),
                pltpu.VMEM((2, 2, LOCAL, BLOCK, GROUP_WIDTH), bf16),
                pltpu.VMEM((2, LOCAL, 6, BLOCK, HEAD), bf16),
                pltpu.VMEM((2, LOCAL, 3, 2, BLOCK, HEAD), bf16),
                pltpu.VMEM((2, LOCAL, 2, BLOCK, HEAD), f32),
                dma((LOCAL, 4)),
                dma((6,)),
                dma((2, LOCAL)),
                dma((2, LOCAL)),
                dma((2, LOCAL, 3, 2)),
                dma((2, LOCAL, 3, 2)),
                dma((2, 2, LOCAL)),
                dma((2, LOCAL)),
                dma((2, LOCAL, 3, 2)),
                dma((2, LOCAL, 3, 2)),
            ],
            compiler_params=pltpu.CompilerParams(
                collective_id=0, has_side_effects=True, vmem_limit_bytes=63 * 2 ** 20),
        )(queries, keys, values, output_gradient, segment_ids.reshape(-1, BLOCK))
        return pl.pallas_call(
            deliver, out_shape=(wide, wide, narrow, narrow), in_specs=[anywhere] * 4, out_specs=(anywhere,) * 4,
            scratch_shapes=[dma((4,))])(*held)

    return jax.shard_map(
        per_device, mesh=mesh, in_specs=(tokens,) * 4 + (P(),), out_specs=(tokens,) * 4, check_vma=False)
```

time: 117 us -> 80.5 us (0.69)
  Pallas kernels: 0 us -> 79.8 us
  starting transfers between devices: 28.4 us -> 0 us
  waiting for transfers between devices: 23.9 us -> 0 us
  matrix products: 21 us -> 0 us
  local copies, waits for them, and re-layouts: 19.5 us -> 0 us
  blocking collectives: 16.6 us -> 0 us
  other arithmetic: 5.33 us -> 0 us
    pallas_call x0 -> x2, Pallas kernels: none -> 79.8 us  [the longest x1 40.8 us: per_device(): pl.pallas_call(deliver, out_shape=(wide, wide, narrow, narrow), in_specs=...]
    ppermute x4 -> x0, waiting for transfers between devices: 22.7 us -> none  [passed_along(): lax.ppermute(value, axis, [(source, source + steps) for source in range(f...]
    dot_general x36 -> x0, matrix products: 21 us -> none  [the longest x6 5.15 us: per_device(): jnp.einsum('gqk,qgd->kd', rounded[distance], grad_group, preferred_elemen...]
    all_to_all x4 -> x0, starting transfers between devices: 16.7 us -> none  [the longest x1 4.4 us: per_device(): lax.all_to_all(query_heads_grad, 'uly', split_axis=0, concat_axis=1, tile...]
    all_to_all x4 -> x0, blocking collectives: 16.6 us -> none  [the longest x1 5.18 us: per_device(): lax.all_to_all(value_heads_grad, 'uly', split_axis=0, concat_axis=1, tile...]
    ppermute x4 -> x0, starting transfers between devices: 11.7 us -> none  [passed_along(): lax.ppermute(value, axis, [(source, source + steps) for source in range(f...]
    unnamed x58 -> x0, local copies, waits for them, and re-layouts: 10.2 us -> none
    all_to_all x5 -> x0, local copies, waits for them, and re-layouts: 3.8 us -> none  [the longest x1 1.57 us: per_device(): lax.all_to_all(keys, 'uly', split_axis=1, concat_axis=0, tiled=True)]
  transfers between devices with their start and end apart: 8 -> 0, of which waited for: 5 -> 0; matrix products, arithmetic and copies ran while one was open for 10% -> 0% of each run, Pallas kernels for 0% -> 0%
where the time goes in v1:
time: 80.5 us; the launch traced here: 80.4 us
  Pallas kernels  79.8 us (99%)
    pallas_call x1, Pallas kernels, per_device(): pl.pallas_call(deliver, out_shape=(wide, wide, narrow, narrow), in_specs=...  40.8 us
    pallas_call x1, Pallas kernels, per_device(): pl.pallas_call(functools.partial(kernel, chips), out_shape=(wide, wide, n...  38.9 us

profile of v1, /device:TPU:255, one launch (start us, length us, event | category | flops | bytes accessed | tf_op | source)
XLA Modules:
  0.0 80.4 jit_solution(6001480526606621238)
XLA Ops:
  0.6 38.9 %shard_map.84 = (bf16[128,2048]{1,0:T(8,128)(2,1)}, bf16[128,2048]{1,0:T(8,128)(2,1)}, bf16[128,512]{1,0:T(8,128)(2,1)}, bf16[128,512]{1,0:T(8,128)(2,1)}) custom-call(bf16[128,2048]{1,0:T(8,128)(2,1)} %q_hbm.1, bf16[128,512]{1,0:T(8,128)(2,1)} %k_hbm.1, bf16[128,512]{1,0:T(8,128)(2,1)} %v_hbm.1, bf16[128,2048]{1,0:T(8,128)(2,1)} %g_hbm.1, s32[512,128]{1,0:T(8,128)} %bitcast.1), custom_call_target="tpu_custom_call" | custom-call | tf_op jit(solution)/shard_map/pallas_call | solution.py:272
  39.5 40.8 %shard_map.85 = (bf16[128,2048]{1,0:T(8,128)(2,1)}, bf16[128,2048]{1,0:T(8,128)(2,1)}, bf16[128,512]{1,0:T(8,128)(2,1)}, bf16[128,512]{1,0:T(8,128)(2,1)}) custom-call(bf16[128,2048]{1,0:T(8,128)(2,1)} %get-tuple-element.8.a0, bf16[128,2048]{1,0:T(8,128)(2,1)} %get-tuple-element.9.a1, bf16[128,512]{1,0:T(8,128)(2,1)} %get-tuple-element.10.a2, ...), custom_call_target="tpu_custom_call" | custom-call | tf_op jit(solution)/shard_map/pallas_call | solution.py:302

commit v2 on v1

v2 whole, which is shorter than its diff:
```python
import functools
import math

import jax
import jax.numpy as jnp
from jax import lax
from jax.experimental import pallas as pl
from jax.experimental.pallas import tpu as pltpu
from jax.sharding import PartitionSpec as P

MESH = pl.DeviceIdType.MESH
HEAD = 128
BLOCK = 128
GROUP = 4
GROUP_WIDTH = GROUP * HEAD
LOCAL = 2
HALF = LOCAL * GROUP_WIDTH
REACH = 2
SPAN = 5
ROWS = SPAN * BLOCK
SCALE = HEAD ** -0.5
TO_EXP2 = SCALE * math.log2(math.e)
NONE = -1e30

f32 = jnp.float32
bf16 = jnp.bfloat16


def dot(a, b, ca, cb):
    return lax.dot_general(a, b, (((ca,), (cb,)), ((), ())), preferred_element_type=f32)


def kernel(chips, q_hbm, k_hbm, v_hbm, g_hbm, ids_hbm, o_hbm, dq_hbm, dk_ref, dv_ref,
           q_buf, g_buf, kv_buf, ids_buf, bias, acc, out_buf, part, got, grad_buf, stage, probs_buf,
           own_sem, stage_sem, ids_sem, qs_send, qs_recv, kv_send, kv_recv, out_sem, out_recv, part_send, part_recv):
    c, u = lax.axis_index("ctx"), lax.axis_index("uly")
    other = 1 - u
    kv_hbm = (k_hbm, v_hbm)

    barrier = pltpu.get_barrier_semaphore()
    pl.semaphore_signal(barrier, inc=1, device_id=(c, other), device_id_type=MESH)
    for step in (1, 2):
        for t in (0, 1):
            @pl.when(c >= step)
            def _():
                pl.semaphore_signal(barrier, inc=1, device_id=(c - step, t), device_id_type=MESH)

            @pl.when(c + step < chips)
            def _():
                pl.semaphore_signal(barrier, inc=1, device_id=(c + step, t), device_id_type=MESH)

    def own_q(i, g):
        columns = pl.ds(pl.multiple_of(u * HALF + g * GROUP_WIDTH, GROUP_WIDTH), GROUP_WIDTH)
        return pltpu.make_async_copy((q_hbm, g_hbm)[i].at[:, columns], (q_buf, g_buf)[i].at[u, g], own_sem.at[g, i])

    def own_kv(i, g):
        narrow = pl.ds(pl.multiple_of((u * LOCAL + g) * HEAD, HEAD), HEAD)
        return pltpu.make_async_copy(kv_hbm[i].at[:, narrow], kv_buf.at[i, g, 4 + u], own_sem.at[g, 2 + i])

    def staged(i, g, t):
        return pltpu.make_async_copy(
            kv_hbm[i].at[:, pl.ds((t * LOCAL + g) * HEAD, HEAD)], stage.at[i, g, t], stage_sem.at[i, g, t])

    ids_copies = []
    for b in range(6):
        row = jnp.maximum(2 * c - 4 + b, 0)
        ids_copies.append(pltpu.make_async_copy(ids_hbm.at[pl.ds(row, 1)], ids_buf.at[b, pl.ds(0, 1)], ids_sem.at[b]))
    for g in range(LOCAL):
        for i in range(2):
            for t in (0, 1):
                staged(i, g, t).start()
    for copy in ids_copies:
        copy.start()
    for g in range(LOCAL):
        for i in range(2):
            own_kv(i, g).start()
            own_q(i, g).start()

    for step in (1, 2):
        for i in range(2):
            @pl.when(c < step)
            def _():
                for g in range(LOCAL):
                    for t in (0, 1):
                        kv_buf[i, g, 2 * (REACH - step) + t] = jnp.zeros((BLOCK, HEAD), bf16)

    heard = 1
    for step in (1, 2):
        heard = heard + 2 * jnp.where(c >= step, 1, 0) + 2 * jnp.where(c + step < chips, 1, 0)
    for g in range(LOCAL):
        for i in range(2):
            for t in (0, 1):
                staged(i, g, t).wait()
    pl.semaphore_wait(barrier, heard)

    def halo(i, g, step, t):
        return pltpu.make_async_remote_copy(
            stage.at[i, g, t], kv_buf.at[i, g, 2 * (REACH - step) + u],
            kv_send.at[i, g, step, t], kv_recv.at[i, g, step, u], device_id=(c + step, t), device_id_type=MESH)

    def swap_kv(i, g):
        return pltpu.make_async_remote_copy(
            stage.at[i, g, other], kv_buf.at[i, g, 4 + u],
            kv_send.at[i, g, 0, 0], kv_recv.at[i, g, 0, 0], device_id=(c, other), device_id_type=MESH)

    def swap_q(i, g):
        columns = pl.ds(pl.multiple_of(other * HALF + g * GROUP_WIDTH, GROUP_WIDTH), GROUP_WIDTH)
        return pltpu.make_async_remote_copy(
            (q_hbm, g_hbm)[i].at[:, columns], (q_buf, g_buf)[i].at[u, g],
            qs_send.at[i, g], qs_recv.at[i, g], device_id=(c, other), device_id_type=MESH)

    def send_halo(i, g):
        for step in (2, 1):
            @pl.when(c + step < chips)
            def _():
                for t in (0, 1):
                    halo(i, g, step, t).start()

    def halo_left(i, g):
        for step in (2, 1):
            @pl.when(c + step < chips)
            def _():
                for t in (0, 1):
                    halo(i, g, step, t).wait_send()

    def halo_here(i, g):
        for step in (1, 2):
            @pl.when(c >= step)
            def _():
                for t in (0, 1):
                    arrived(i, g, step, t).wait_recv()

    for i in range(2):
        send_halo(i, 0)
    for g in range(LOCAL):
        swap_kv(0, g).start()
        for i in range(2):
            swap_q(i, g).start()
        swap_kv(1, g).start()

    for copy in ids_copies:
        copy.wait()
    below = lax.broadcasted_iota(jnp.int32, (BLOCK, BLOCK), 0) <= lax.broadcasted_iota(jnp.int32, (BLOCK, BLOCK), 1)
    for b in range(6):
        key_ids = jnp.transpose(jnp.broadcast_to(ids_buf[b, 0:1, :], (BLOCK, BLOCK)))
        if b < 4:
            key_ids = jnp.where(c >= REACH - b // 2, key_ids, -1)
        for s in (0, 1):
            if not s <= b < s + SPAN:
                continue
            allowed = key_ids == jnp.broadcast_to(ids_buf[4 + s, 0:1, :], (BLOCK, BLOCK))
            if b == 4 + s:
                allowed = allowed & below
            bias[s, b - s] = jnp.where(allowed, 0.0, NONE)

    halo_left(0, 0)
    send_halo(0, 1)

    def out_local(i, s, g):
        columns = pl.ds(pl.multiple_of(u * HALF + g * GROUP_WIDTH, GROUP_WIDTH), GROUP_WIDTH)
        return pltpu.make_async_copy(out_buf.at[i, s, g], (o_hbm, dq_hbm)[i].at[:, columns], out_sem.at[i, 0, g])

    def out_remote(i, s, g):
        columns = pl.ds(pl.multiple_of(u * HALF + g * GROUP_WIDTH, GROUP_WIDTH), GROUP_WIDTH)
        return pltpu.make_async_remote_copy(
            out_buf.at[i, s, g], (o_hbm, dq_hbm)[i].at[:, columns],
            out_sem.at[i, 1, g], out_recv.at[i, g], device_id=(c, other), device_id_type=MESH)

    def partial(i, g, step, t):
        return pltpu.make_async_remote_copy(
            part.at[i, g, 2 * (REACH - step) + t], got.at[i, g, step, u],
            part_send.at[i, g, step, t], part_recv.at[i, g, step, u], device_id=(c - step, t), device_id_type=MESH)

    def partial_chip(i, g):
        return pltpu.make_async_remote_copy(
            part.at[i, g, 4 + other], got.at[i, g, 0, u],
            part_send.at[i, g, 0, 0], part_recv.at[i, g, 0, 0], device_id=(c, other), device_id_type=MESH)

    def pairs(g, s):
        for pair in range(GROUP // 2):
            heads = [slice((2 * pair + h) * HEAD, (2 * pair + h + 1) * HEAD) for h in (0, 1)]
            yield pair, heads, [jnp.concatenate([buf[s, g, :, h] for h in heads], axis=0) for buf in (q_buf, g_buf)]

    def first(g, s):
        keys = kv_buf[0, g, pl.ds(s, SPAN)].reshape(ROWS, HEAD)
        add = bias[s].reshape(ROWS, BLOCK)
        add = jnp.concatenate([add, add], axis=1)
        dv = jnp.zeros((ROWS, HEAD), f32)
        for pair, heads, (qs, gs) in pairs(g, s):
            scores = dot(keys, qs, 1, 1) * TO_EXP2 + add
            probs = jnp.exp2(scores - jnp.max(scores, axis=0, keepdims=True))
            probs = (probs * (1.0 / jnp.sum(probs, axis=0, keepdims=True))).astype(bf16)
            probs_buf[s, pair] = probs
            dv = dv + dot(probs, gs, 1, 0)
        acc[1, pl.ds(s, SPAN)] += dv.reshape(SPAN, BLOCK, HEAD)

    def second(g, s):
        keys = kv_buf[0, g, pl.ds(s, SPAN)].reshape(ROWS, HEAD)
        vals = kv_buf[1, g, pl.ds(s, SPAN)].reshape(ROWS, HEAD)
        keys_t, vals_t = jnp.transpose(keys), jnp.transpose(vals)
        dk = jnp.zeros((ROWS, HEAD), f32)
        for pair, heads, (qs, gs) in pairs(g, s):
            rounded = probs_buf[s, pair]
            probs = rounded.astype(f32)
            dprobs = dot(vals, gs, 1, 1)
            delta = jnp.sum(probs * dprobs, axis=0, keepdims=True)
            dscores = (probs * (dprobs - delta)).astype(bf16)
            dk = dk + dot(dscores, qs, 1, 0)
            out_t = dot(vals_t, rounded, 1, 0)
            dq_t = dot(keys_t, dscores, 1, 0) * SCALE
            for h in (0, 1):
                out_buf[0, s, g, :, heads[h]] = jnp.transpose(out_t[:, h * BLOCK:(h + 1) * BLOCK]).astype(bf16)
                out_buf[1, s, g, :, heads[h]] = jnp.transpose(dq_t[:, h * BLOCK:(h + 1) * BLOCK]).astype(bf16)
        acc[0, pl.ds(s, SPAN)] += dk.reshape(SPAN, BLOCK, HEAD) * SCALE

    def send_partials(i, g):
        part[i, g] = acc[i].astype(bf16)
        for step in (2, 1):
            @pl.when(c >= step)
            def _():
                for t in (0, 1):
                    partial(i, g, step, t).start()
        partial_chip(i, g).start()
        grad_buf[i, g, u] = acc[i, 4 + u]

    def head(g, carry):
        for i in range(2):
            own_q(i, g).wait()
            own_kv(i, g).wait()
        swap_kv(0, g).wait_recv()
        for i in range(2):
            swap_q(i, g).wait_recv()
        acc[...] = jnp.zeros(acc.shape, f32)
        halo_here(0, g)
        first(g, other)
        first(g, u)
        send_partials(1, g)

        @pl.when(g == 0)
        def _():
            halo_left(1, 0)
            send_halo(1, 1)

        swap_kv(1, g).wait_recv()
        halo_here(1, g)
        second(g, other)
        for i in range(2):
            out_remote(i, other, g).start()
        second(g, u)
        send_partials(0, g)
        for i in range(2):
            out_local(i, u, g).start()
        return carry

    def arrived(i, g, step, t):
        return pltpu.make_async_remote_copy(
            stage.at[i, g, 0], kv_buf.at[i, g, 2 * (REACH - step) + t],
            kv_send.at[i, g, step, t], kv_recv.at[i, g, step, t], device_id=(c, other), device_id_type=MESH)

    def later(i, g, step, t):
        return pltpu.make_async_remote_copy(
            part.at[i, g, 0], got.at[i, g, step, t], part_send.at[i, g, step, t],
            part_recv.at[i, g, step, t], device_id=(c, other), device_id_type=MESH)

    lax.fori_loop(0, LOCAL, head, 0)

    for g in range(LOCAL):
        for i in (1, 0):
            partial_chip(i, g).wait_recv()
            grad_buf[i, g, other] = got[i, g, 0, other].astype(f32)
            for step in (1, 2):
                @pl.when(c + step < chips)
                def _():
                    for t in (0, 1):
                        later(i, g, step, t).wait_recv()
                        grad_buf[i, g, t] += got[i, g, step, t].astype(f32)
            for t in (0, 1):
                (dk_ref, dv_ref)[i][:, (t * LOCAL + g) * HEAD:(t * LOCAL + g + 1) * HEAD] = grad_buf[i, g, t].astype(bf16)

    for i in range(2):
        halo_left(i, 1)
    for g in range(LOCAL):
        for i in range(2):
            out_remote(i, other, g).wait()
            out_local(i, u, g).wait()
            swap_kv(i, g).wait_send()
            swap_q(i, g).wait_send()
            partial_chip(i, g).wait_send()
        for step in (1, 2):
            @pl.when(c >= step)
            def _():
                for i in range(2):
                    for t in (0, 1):
                        partial(i, g, step, t).wait_send()


def deliver(a0, a1, a2, a3, b0, b1, b2, b3, sem):
    copies = [pltpu.make_async_copy(a, b, sem.at[i]) for i, (a, b) in enumerate(zip((a0, a1, a2, a3), (b0, b1, b2, b3)))]
    for copy in copies:
        copy.start()
    for copy in copies:
        copy.wait()


def solution(mesh):
    chips = mesh.shape["ctx"]
    tokens = P(("ctx", "uly"), None)

    def per_device(queries, keys, values, output_gradient, segment_ids):
        rows = queries.shape[0]
        wide = jax.ShapeDtypeStruct((rows, 2 * HALF), bf16)
        narrow = jax.ShapeDtypeStruct((rows, 2 * LOCAL * HEAD), bf16)
        anywhere = pl.BlockSpec(memory_space=pltpu.HBM)
        vmem = pl.BlockSpec(memory_space=pltpu.VMEM)
        dma = pltpu.SemaphoreType.DMA
        held = pl.pallas_call(
            functools.partial(kernel, chips),
            out_shape=tuple(pltpu.VMEM(x.shape, x.dtype) for x in (wide, wide, narrow, narrow)),
            in_specs=[anywhere] * 5,
            out_specs=(vmem,) * 4,
            scratch_shapes=[
                pltpu.VMEM((2, LOCAL, BLOCK, GROUP_WIDTH), bf16),
                pltpu.VMEM((2, LOCAL, BLOCK, GROUP_WIDTH), bf16),
                pltpu.VMEM((2, LOCAL, 6, BLOCK, HEAD), bf16),
                pltpu.VMEM((6, 8, BLOCK), jnp.int32),
                pltpu.VMEM((2, SPAN, BLOCK, BLOCK), f32),
                pltpu.VMEM((2, 6, BLOCK, HEAD), f32),
                pltpu.VMEM((2, 2, LOCAL, BLOCK, GROUP_WIDTH), bf16),
                pltpu.VMEM((2, LOCAL, 6, BLOCK, HEAD), bf16),
                pltpu.VMEM((2, LOCAL, 3, 2, BLOCK, HEAD), bf16),
                pltpu.VMEM((2, LOCAL, 2, BLOCK, HEAD), f32),
                pltpu.VMEM((2, LOCAL, 2, BLOCK, HEAD), bf16),
                pltpu.VMEM((2, GROUP // 2, ROWS, 2 * BLOCK), bf16),
                dma((LOCAL, 4)),
                dma((2, LOCAL, 2)),
                dma((6,)),
                dma((2, LOCAL)),
                dma((2, LOCAL)),
                dma((2, LOCAL, 3, 2)),
                dma((2, LOCAL, 3, 2)),
                dma((2, 2, LOCAL)),
                dma((2, LOCAL)),
                dma((2, LOCAL, 3, 2)),
                dma((2, LOCAL, 3, 2)),
            ],
            compiler_params=pltpu.CompilerParams(
                collective_id=0, has_side_effects=True, vmem_limit_bytes=48 * 2 ** 20),
        )(*[pltpu.with_memory_space_constraint(x, pltpu.HBM) for x in (
            queries, keys, values, output_gradient, segment_ids.reshape(-1, BLOCK))])
        return pl.pallas_call(
            deliver, out_shape=(wide, wide, narrow, narrow), in_specs=[vmem] * 4, out_specs=(anywhere,) * 4,
            scratch_shapes=[dma((4,))], compiler_params=pltpu.CompilerParams(vmem_limit_bytes=2 ** 20))(
                *[pltpu.with_memory_space_constraint(x, pltpu.VMEM) for x in held])

    return jax.shard_map(
        per_device, mesh=mesh, in_specs=(tokens,) * 4 + (P(),), out_specs=(tokens,) * 4, check_vma=False)
```

time: 80.5 us -> 34.3 us (0.43)
  Pallas kernels: 79.8 us -> 33.5 us
    pallas_call x1, Pallas kernels: 40.8 us -> 1.08 us  [per_device(): pl.pallas_call(deliver, out_shape=(wide, wide, narrow, narrow), in_specs=...]
    pallas_call x1, Pallas kernels: 38.9 us -> 32.5 us  [per_device(): pl.pallas_call(functools.partial(kernel, chips), out_shape=tuple((pltpu.V...]
where the time goes in v2:
time: 34.3 us; the launch traced here: 34.2 us
  Pallas kernels  33.5 us (98%)
  between operations  0.64 us (2%)
    pallas_call x1, Pallas kernels, per_device(): pl.pallas_call(functools.partial(kernel, chips), out_shape=tuple((pltpu.V...  32.5 us
    pallas_call x1, Pallas kernels, per_device(): pl.pallas_call(deliver, out_shape=(wide, wide, narrow, narrow), in_specs=...  1.08 us

profile of v2, /device:TPU:255, one launch (start us, length us, event | category | flops | bytes accessed | tf_op | source)
XLA Modules:
  0.0 34.2 jit_solution(5622560321902383033)
XLA Ops:
  0.6 32.5 %shard_map.84 = (bf16[128,2048]{1,0:T(8,128)(2,1)S(1)}, bf16[128,2048]{1,0:T(8,128)(2,1)S(1)}, bf16[128,512]{1,0:T(8,128)(2,1)S(1)}, bf16[128,512]{1,0:T(8,128)(2,1)S(1)}) custom-call(bf16[128,2048]{1,0:T(8,128)(2,1)} %q_hbm.1, bf16[128,512]{1,0:T(8,128)(2,1)} %k_hbm.1, bf16[128,512]{1,0:T(8,128)(2,1)} %v_hbm.1, bf16[128,2048]{1,0:T(8,128)(2,1)} %g_hbm.1, ...), custom_call_target="tpu_custom_call" | custom-call | tf_op jit(solution)/shard_map/pallas_call | solution.py:316
  33.1 1.1 %shard_map.85 = (bf16[128,2048]{1,0:T(8,128)(2,1)}, bf16[128,2048]{1,0:T(8,128)(2,1)}, bf16[128,512]{1,0:T(8,128)(2,1)}, bf16[128,512]{1,0:T(8,128)(2,1)}) custom-call(bf16[128,2048]{1,0:T(8,128)(2,1)S(1)} %get-tuple-element.8.a0, bf16[128,2048]{1,0:T(8,128)(2,1)S(1)} %get-tuple-element.9.a1, bf16[128,512]{1,0:T(8,128)(2,1)S(1)} %get-tuple-element.10.a2, ...), custom_call_target="tpu_custom_call" | custom-call | tf_op jit(solution)/shard_map/pallas_call | solution.py:350

commit v3 on v2

--- a/solution.py
+++ b/solution.py
@@ -31,7 +31,7 @@
 
 
 def kernel(chips, q_hbm, k_hbm, v_hbm, g_hbm, ids_hbm, o_hbm, dq_hbm, dk_ref, dv_ref,
-           q_buf, g_buf, kv_buf, ids_buf, bias, acc, out_buf, part, got, grad_buf, stage, probs_buf,
+           q_buf, g_buf, kv_buf, ids_buf, bias, acc, out_buf, part, got, grad_buf, stage, probs_buf, dscores_buf,
            own_sem, stage_sem, ids_sem, qs_send, qs_recv, kv_send, kv_recv, out_sem, out_recv, part_send, part_recv):
     c, u = lax.axis_index("ctx"), lax.axis_index("uly")
     other = 1 - u
@@ -110,7 +110,7 @@
             qs_send.at[i, g], qs_recv.at[i, g], device_id=(c, other), device_id_type=MESH)
 
     def send_halo(i, g):
-        for step in (2, 1):
+        for step in (1, 2):
             @pl.when(c + step < chips)
             def _():
                 for t in (0, 1):
@@ -190,28 +190,32 @@
             scores = dot(keys, qs, 1, 1) * TO_EXP2 + add
             probs = jnp.exp2(scores - jnp.max(scores, axis=0, keepdims=True))
             probs = (probs * (1.0 / jnp.sum(probs, axis=0, keepdims=True))).astype(bf16)
-            probs_buf[s, pair] = probs
+            probs_buf[g, s, pair] = probs
             dv = dv + dot(probs, gs, 1, 0)
         acc[1, pl.ds(s, SPAN)] += dv.reshape(SPAN, BLOCK, HEAD)
 
     def second(g, s):
-        keys = kv_buf[0, g, pl.ds(s, SPAN)].reshape(ROWS, HEAD)
         vals = kv_buf[1, g, pl.ds(s, SPAN)].reshape(ROWS, HEAD)
-        keys_t, vals_t = jnp.transpose(keys), jnp.transpose(vals)
         dk = jnp.zeros((ROWS, HEAD), f32)
         for pair, heads, (qs, gs) in pairs(g, s):
-            rounded = probs_buf[s, pair]
-            probs = rounded.astype(f32)
+            probs = probs_buf[g, s, pair].astype(f32)
             dprobs = dot(vals, gs, 1, 1)
             delta = jnp.sum(probs * dprobs, axis=0, keepdims=True)
             dscores = (probs * (dprobs - delta)).astype(bf16)
+            dscores_buf[g, s, pair] = dscores
             dk = dk + dot(dscores, qs, 1, 0)
-            out_t = dot(vals_t, rounded, 1, 0)
-            dq_t = dot(keys_t, dscores, 1, 0) * SCALE
+        acc[0, pl.ds(s, SPAN)] += dk.reshape(SPAN, BLOCK, HEAD) * SCALE
+
+    def third(g, s):
+        keys_t = jnp.transpose(kv_buf[0, g, pl.ds(s, SPAN)].reshape(ROWS, HEAD))
+        vals_t = jnp.transpose(kv_buf[1, g, pl.ds(s, SPAN)].reshape(ROWS, HEAD))
+        for pair in range(GROUP // 2):
+            out_t = dot(vals_t, probs_buf[g, s, pair], 1, 0)
+            dq_t = dot(keys_t, dscores_buf[g, s, pair], 1, 0) * SCALE
             for h in (0, 1):
-                out_buf[0, s, g, :, heads[h]] = jnp.transpose(out_t[:, h * BLOCK:(h + 1) * BLOCK]).astype(bf16)
-                out_buf[1, s, g, :, heads[h]] = jnp.transpose(dq_t[:, h * BLOCK:(h + 1) * BLOCK]).astype(bf16)
-        acc[0, pl.ds(s, SPAN)] += dk.reshape(SPAN, BLOCK, HEAD) * SCALE
+                head = slice((2 * pair + h) * HEAD, (2 * pair + h + 1) * HEAD)
+                out_buf[0, s, g, :, head] = jnp.transpose(out_t[:, h * BLOCK:(h + 1) * BLOCK]).astype(bf16)
+                out_buf[1, s, g, :, head] = jnp.transpose(dq_t[:, h * BLOCK:(h + 1) * BLOCK]).astype(bf16)
 
     def send_partials(i, g):
         part[i, g] = acc[i].astype(bf16)
@@ -244,10 +248,15 @@
         swap_kv(1, g).wait_recv()
         halo_here(1, g)
         second(g, other)
-        for i in range(2):
-            out_remote(i, other, g).start()
         second(g, u)
         send_partials(0, g)
+        return carry
+
+    def rest(g, carry):
+        third(g, other)
+        for i in range(2):
+            out_remote(i, other, g).start()
+        third(g, u)
         for i in range(2):
             out_local(i, u, g).start()
         return carry
@@ -263,6 +272,7 @@
             part_recv.at[i, g, step, t], device_id=(c, other), device_id_type=MESH)
 
     lax.fori_loop(0, LOCAL, head, 0)
+    lax.fori_loop(0, LOCAL, rest, 0)
 
     for g in range(LOCAL):
         for i in (1, 0):
@@ -330,7 +340,8 @@
                 pltpu.VMEM((2, LOCAL, 3, 2, BLOCK, HEAD), bf16),
                 pltpu.VMEM((2, LOCAL, 2, BLOCK, HEAD), f32),
                 pltpu.VMEM((2, LOCAL, 2, BLOCK, HEAD), bf16),
-                pltpu.VMEM((2, GROUP // 2, ROWS, 2 * BLOCK), bf16),
+                pltpu.VMEM((LOCAL, 2, GROUP // 2, ROWS, 2 * BLOCK), bf16),
+                pltpu.VMEM((LOCAL, 2, GROUP // 2, ROWS, 2 * BLOCK), bf16),
                 dma((LOCAL, 4)),
                 dma((2, LOCAL, 2)),
                 dma((6,)),

time: 34.3 us -> 35.1 us (1.023)
  the two profiles are of different devices: /device:TPU:255 before, /device:TPU:259 now
where the time goes in v3:
time: 35.1 us; the launch traced here: 35 us
  Pallas kernels  34.3 us (98%)
  between operations  0.64 us (2%)
    pallas_call x1, Pallas kernels, per_device(): pl.pallas_call(functools.partial(kernel, chips), out_shape=tuple((pltpu.V...  33.2 us
    pallas_call x1, Pallas kernels, per_device(): pl.pallas_call(deliver, out_shape=(wide, wide, narrow, narrow), in_specs=...  1.08 us

profile of v3, /device:TPU:259, one launch (start us, length us, event | category | flops | bytes accessed | tf_op | source)
XLA Modules:
  0.0 35.0 jit_solution(17391343169842962325)
XLA Ops:
  0.6 33.2 %shard_map.84 = (bf16[128,2048]{1,0:T(8,128)(2,1)S(1)}, bf16[128,2048]{1,0:T(8,128)(2,1)S(1)}, bf16[128,512]{1,0:T(8,128)(2,1)S(1)}, bf16[128,512]{1,0:T(8,128)(2,1)S(1)}) custom-call(bf16[128,2048]{1,0:T(8,128)(2,1)} %q_hbm.1, bf16[128,512]{1,0:T(8,128)(2,1)} %k_hbm.1, bf16[128,512]{1,0:T(8,128)(2,1)} %v_hbm.1, bf16[128,2048]{1,0:T(8,128)(2,1)} %g_hbm.1, ...), custom_call_target="tpu_custom_call" | custom-call | tf_op jit(solution)/shard_map/pallas_call | solution.py:326
  33.9 1.1 %shard_map.85 = (bf16[128,2048]{1,0:T(8,128)(2,1)}, bf16[128,2048]{1,0:T(8,128)(2,1)}, bf16[128,512]{1,0:T(8,128)(2,1)}, bf16[128,512]{1,0:T(8,128)(2,1)}) custom-call(bf16[128,2048]{1,0:T(8,128)(2,1)S(1)} %get-tuple-element.8.a0, bf16[128,2048]{1,0:T(8,128)(2,1)S(1)} %get-tuple-element.9.a1, bf16[128,512]{1,0:T(8,128)(2,1)S(1)} %get-tuple-element.10.a2, ...), custom_call_target="tpu_custom_call" | custom-call | tf_op jit(solution)/shard_map/pallas_call | solution.py:361

commit v4 on v3

--- a/solution.py
+++ b/solution.py
@@ -16,6 +16,7 @@
 LOCAL = 2
 HALF = LOCAL * GROUP_WIDTH
 REACH = 2
+RING = 4
 SPAN = 5
 ROWS = SPAN * BLOCK
 SCALE = HEAD ** -0.5
@@ -36,6 +37,8 @@
     c, u = lax.axis_index("ctx"), lax.axis_index("uly")
     other = 1 - u
     kv_hbm = (k_hbm, v_hbm)
+    odd = lax.rem(c, 2) == 1
+    first_x = lax.rem(c, RING) == 0
 
     barrier = pltpu.get_barrier_semaphore()
     pl.semaphore_signal(barrier, inc=1, device_id=(c, other), device_id_type=MESH)
@@ -110,11 +113,15 @@
             qs_send.at[i, g], qs_recv.at[i, g], device_id=(c, other), device_id_type=MESH)
 
     def send_halo(i, g):
-        for step in (1, 2):
-            @pl.when(c + step < chips)
+        def to(step, when):
+            @pl.when(when & (c + step < chips))
             def _():
                 for t in (0, 1):
                     halo(i, g, step, t).start()
+
+        to(1, odd)
+        to(2, c >= 0)
+        to(1, ~odd)
 
     def halo_left(i, g):
         for step in (2, 1):
@@ -130,8 +137,9 @@
                 for t in (0, 1):
                     arrived(i, g, step, t).wait_recv()
 
-    for i in range(2):
-        send_halo(i, 0)
+    for g in range(LOCAL):
+        for i in range(2):
+            send_halo(i, g)
     for g in range(LOCAL):
         swap_kv(0, g).start()
         for i in range(2):
@@ -153,8 +161,6 @@
                 allowed = allowed & below
             bias[s, b - s] = jnp.where(allowed, 0.0, NONE)
 
-    halo_left(0, 0)
-    send_halo(0, 1)
 
     def out_local(i, s, g):
         columns = pl.ds(pl.multiple_of(u * HALF + g * GROUP_WIDTH, GROUP_WIDTH), GROUP_WIDTH)
@@ -219,11 +225,15 @@
 
     def send_partials(i, g):
         part[i, g] = acc[i].astype(bf16)
-        for step in (2, 1):
-            @pl.when(c >= step)
+        def to(step, when):
+            @pl.when(when & (c >= step))
             def _():
                 for t in (0, 1):
                     partial(i, g, step, t).start()
+
+        to(1, first_x)
+        to(2, c >= 0)
+        to(1, ~first_x)
         partial_chip(i, g).start()
         grad_buf[i, g, u] = acc[i, 4 + u]
 
@@ -239,11 +249,6 @@
         first(g, other)
         first(g, u)
         send_partials(1, g)
-
-        @pl.when(g == 0)
-        def _():
-            halo_left(1, 0)
-            send_halo(1, 1)
 
         swap_kv(1, g).wait_recv()
         halo_here(1, g)
@@ -288,7 +293,8 @@
                 (dk_ref, dv_ref)[i][:, (t * LOCAL + g) * HEAD:(t * LOCAL + g + 1) * HEAD] = grad_buf[i, g, t].astype(bf16)
 
     for i in range(2):
-        halo_left(i, 1)
+        for g in range(LOCAL):
+            halo_left(i, g)
     for g in range(LOCAL):
         for i in range(2):
             out_remote(i, other, g).wait()

time: 35.1 us -> 33.3 us (0.949)
  the two profiles are of different devices: /device:TPU:259 before, /device:TPU:253 now
where the time goes in v4:
time: 33.3 us; the launch traced here: 33.2 us
  Pallas kernels  32.6 us (98%)
  between operations  0.64 us (2%)
    pallas_call x1, Pallas kernels, per_device(): pl.pallas_call(functools.partial(kernel, chips), out_shape=tuple((pltpu.V...  31.5 us
    pallas_call x1, Pallas kernels, per_device(): pl.pallas_call(deliver, out_shape=(wide, wide, narrow, narrow), in_specs=...  1.08 us

profile of v4, /device:TPU:253, one launch (start us, length us, event | category | flops | bytes accessed | tf_op | source)
XLA Modules:
  0.0 33.2 jit_solution(1277026926702571348)
XLA Ops:
  0.6 31.5 %shard_map.84 = (bf16[128,2048]{1,0:T(8,128)(2,1)S(1)}, bf16[128,2048]{1,0:T(8,128)(2,1)S(1)}, bf16[128,512]{1,0:T(8,128)(2,1)S(1)}, bf16[128,512]{1,0:T(8,128)(2,1)S(1)}) custom-call(bf16[128,2048]{1,0:T(8,128)(2,1)} %q_hbm.1, bf16[128,512]{1,0:T(8,128)(2,1)} %k_hbm.1, bf16[128,512]{1,0:T(8,128)(2,1)} %v_hbm.1, bf16[128,2048]{1,0:T(8,128)(2,1)} %g_hbm.1, ...), custom_call_target="tpu_custom_call" | custom-call | tf_op jit(solution)/shard_map/pallas_call | solution.py:332
  32.1 1.1 %shard_map.85 = (bf16[128,2048]{1,0:T(8,128)(2,1)}, bf16[128,2048]{1,0:T(8,128)(2,1)}, bf16[128,512]{1,0:T(8,128)(2,1)}, bf16[128,512]{1,0:T(8,128)(2,1)}) custom-call(bf16[128,2048]{1,0:T(8,128)(2,1)S(1)} %get-tuple-element.8.a0, bf16[128,2048]{1,0:T(8,128)(2,1)S(1)} %get-tuple-element.9.a1, bf16[128,512]{1,0:T(8,128)(2,1)S(1)} %get-tuple-element.10.a2, ...), custom_call_target="tpu_custom_call" | custom-call | tf_op jit(solution)/shard_map/pallas_call | solution.py:367

commit v5 on v4

--- a/solution.py
+++ b/solution.py
@@ -48,10 +48,6 @@
             def _():
                 pl.semaphore_signal(barrier, inc=1, device_id=(c - step, t), device_id_type=MESH)
 
-            @pl.when(c + step < chips)
-            def _():
-                pl.semaphore_signal(barrier, inc=1, device_id=(c + step, t), device_id_type=MESH)
-
     def own_q(i, g):
         columns = pl.ds(pl.multiple_of(u * HALF + g * GROUP_WIDTH, GROUP_WIDTH), GROUP_WIDTH)
         return pltpu.make_async_copy((q_hbm, g_hbm)[i].at[:, columns], (q_buf, g_buf)[i].at[u, g], own_sem.at[g, i])
@@ -89,7 +85,7 @@
 
     heard = 1
     for step in (1, 2):
-        heard = heard + 2 * jnp.where(c >= step, 1, 0) + 2 * jnp.where(c + step < chips, 1, 0)
+        heard = heard + 2 * jnp.where(c + step < chips, 1, 0)
     for g in range(LOCAL):
         for i in range(2):
             for t in (0, 1):

time: 33.3 us -> 33.3 us (level)
  the two profiles are of different devices: /device:TPU:253 before, /device:TPU:255 now
where the time goes in v5:
time: 33.3 us; the launch traced here: 33.2 us
  Pallas kernels  32.5 us (98%)
  between operations  0.64 us (2%)
    pallas_call x1, Pallas kernels, per_device(): pl.pallas_call(functools.partial(kernel, chips), out_shape=tuple((pltpu.V...  31.4 us
    pallas_call x1, Pallas kernels, per_device(): pl.pallas_call(deliver, out_shape=(wide, wide, narrow, narrow), in_specs=...  1.08 us

profile of v5, /device:TPU:255, one launch (start us, length us, event | category | flops | bytes accessed | tf_op | source)
XLA Modules:
  0.0 33.2 jit_solution(11132903769490371084)
XLA Ops:
  0.6 31.4 %shard_map.84 = (bf16[128,2048]{1,0:T(8,128)(2,1)S(1)}, bf16[128,2048]{1,0:T(8,128)(2,1)S(1)}, bf16[128,512]{1,0:T(8,128)(2,1)S(1)}, bf16[128,512]{1,0:T(8,128)(2,1)S(1)}) custom-call(bf16[128,2048]{1,0:T(8,128)(2,1)} %q_hbm.1, bf16[128,512]{1,0:T(8,128)(2,1)} %k_hbm.1, bf16[128,512]{1,0:T(8,128)(2,1)} %v_hbm.1, bf16[128,2048]{1,0:T(8,128)(2,1)} %g_hbm.1, ...), custom_call_target="tpu_custom_call" | custom-call | tf_op jit(solution)/shard_map/pallas_call | solution.py:328
  32.1 1.1 %shard_map.85 = (bf16[128,2048]{1,0:T(8,128)(2,1)}, bf16[128,2048]{1,0:T(8,128)(2,1)}, bf16[128,512]{1,0:T(8,128)(2,1)}, bf16[128,512]{1,0:T(8,128)(2,1)}) custom-call(bf16[128,2048]{1,0:T(8,128)(2,1)S(1)} %get-tuple-element.8.a0, bf16[128,2048]{1,0:T(8,128)(2,1)S(1)} %get-tuple-element.9.a1, bf16[128,512]{1,0:T(8,128)(2,1)S(1)} %get-tuple-element.10.a2, ...), custom_call_target="tpu_custom_call" | custom-call | tf_op jit(solution)/shard_map/pallas_call | solution.py:363

commit v6 on v5

--- a/solution.py
+++ b/solution.py
@@ -220,7 +220,7 @@
                 out_buf[1, s, g, :, head] = jnp.transpose(dq_t[:, h * BLOCK:(h + 1) * BLOCK]).astype(bf16)
 
     def send_partials(i, g):
-        part[i, g] = acc[i].astype(bf16)
+        part[i, g, 0:4] = acc[i, 0:4].astype(bf16)
         def to(step, when):
             @pl.when(when & (c >= step))
             def _():
@@ -230,6 +230,7 @@
         to(1, first_x)
         to(2, c >= 0)
         to(1, ~first_x)
+        part[i, g, 4:6] = acc[i, 4:6].astype(bf16)
         partial_chip(i, g).start()
         grad_buf[i, g, u] = acc[i, 4 + u]
 
@@ -275,35 +276,38 @@
     lax.fori_loop(0, LOCAL, head, 0)
     lax.fori_loop(0, LOCAL, rest, 0)
 
-    for g in range(LOCAL):
-        for i in (1, 0):
-            partial_chip(i, g).wait_recv()
-            grad_buf[i, g, other] = got[i, g, 0, other].astype(f32)
-            for step in (1, 2):
-                @pl.when(c + step < chips)
-                def _():
-                    for t in (0, 1):
-                        later(i, g, step, t).wait_recv()
-                        grad_buf[i, g, t] += got[i, g, step, t].astype(f32)
-            for t in (0, 1):
-                (dk_ref, dv_ref)[i][:, (t * LOCAL + g) * HEAD:(t * LOCAL + g + 1) * HEAD] = grad_buf[i, g, t].astype(bf16)
-
-    for i in range(2):
-        for g in range(LOCAL):
+    def collect(i, g):
+        partial_chip(i, g).wait_recv()
+        grad_buf[i, g, other] = got[i, g, 0, other].astype(f32)
+        for step in (1, 2):
+            @pl.when(c + step < chips)
+            def _():
+                for t in (0, 1):
+                    later(i, g, step, t).wait_recv()
+                    grad_buf[i, g, t] += got[i, g, step, t].astype(f32)
+        for t in (0, 1):
+            (dk_ref, dv_ref)[i][:, (t * LOCAL + g) * HEAD:(t * LOCAL + g + 1) * HEAD] = grad_buf[i, g, t].astype(bf16)
+
+    def partials_left(i, g):
+        partial_chip(i, g).wait_send()
+        for step in (1, 2):
+            @pl.when(c >= step)
+            def _():
+                for t in (0, 1):
+                    partial(i, g, step, t).wait_send()
+
+    for g in range(LOCAL):
+        for i in range(2):
             halo_left(i, g)
+            swap_kv(i, g).wait_send()
+            swap_q(i, g).wait_send()
     for g in range(LOCAL):
         for i in range(2):
             out_remote(i, other, g).wait()
             out_local(i, u, g).wait()
-            swap_kv(i, g).wait_send()
-            swap_q(i, g).wait_send()
-            partial_chip(i, g).wait_send()
-        for step in (1, 2):
-            @pl.when(c >= step)
-            def _():
-                for i in range(2):
-                    for t in (0, 1):
-                        partial(i, g, step, t).wait_send()
+    for i, g in ((1, 0), (0, 0), (1, 1), (0, 1)):
+        partials_left(i, g)
+        collect(i, g)
 
 
 def deliver(a0, a1, a2, a3, b0, b1, b2, b3, sem):

time: 33.3 us -> 33.2 us (level)
  no operation moved by 1% of the time
where the time goes in v6:
time: 33.2 us; the launch traced here: 33.1 us
  Pallas kernels  32.4 us (98%)
  between operations  0.64 us (2%)
    pallas_call x1, Pallas kernels, per_device(): pl.pallas_call(functools.partial(kernel, chips), out_shape=tuple((pltpu.V...  31.3 us
    pallas_call x1, Pallas kernels, per_device(): pl.pallas_call(deliver, out_shape=(wide, wide, narrow, narrow), in_specs=...  1.08 us

profile of v6, /device:TPU:255, one launch (start us, length us, event | category | flops | bytes accessed | tf_op | source)
XLA Modules:
  0.0 33.1 jit_solution(17091431691355300727)
XLA Ops:
  0.6 31.3 %shard_map.84 = (bf16[128,2048]{1,0:T(8,128)(2,1)S(1)}, bf16[128,2048]{1,0:T(8,128)(2,1)S(1)}, bf16[128,512]{1,0:T(8,128)(2,1)S(1)}, bf16[128,512]{1,0:T(8,128)(2,1)S(1)}) custom-call(bf16[128,2048]{1,0:T(8,128)(2,1)} %q_hbm.1, bf16[128,512]{1,0:T(8,128)(2,1)} %k_hbm.1, bf16[128,512]{1,0:T(8,128)(2,1)} %v_hbm.1, bf16[128,2048]{1,0:T(8,128)(2,1)} %g_hbm.1, ...), custom_call_target="tpu_custom_call" | custom-call | tf_op jit(solution)/shard_map/pallas_call | solution.py:332
  32.0 1.1 %shard_map.85 = (bf16[128,2048]{1,0:T(8,128)(2,1)}, bf16[128,2048]{1,0:T(8,128)(2,1)}, bf16[128,512]{1,0:T(8,128)(2,1)}, bf16[128,512]{1,0:T(8,128)(2,1)}) custom-call(bf16[128,2048]{1,0:T(8,128)(2,1)S(1)} %get-tuple-element.8.a0, bf16[128,2048]{1,0:T(8,128)(2,1)S(1)} %get-tuple-element.9.a1, bf16[128,512]{1,0:T(8,128)(2,1)S(1)} %get-tuple-element.10.a2, ...), custom_call_target="tpu_custom_call" | custom-call | tf_op jit(solution)/shard_map/pallas_call | solution.py:367
